TPU v7x, 512 devices: a whole 4x4x16 slice. The times are simulated.
512 devices in a mesh: island: 8 (over y, x_hi), fsdp: 64 (over z, x_lo, core).
Axes of the slice: x: 4 (x_hi: 2, x_lo: 2; x = x_hi * 2 + x_lo), y: 4, z: 16, core: 2. Of those that a mesh axis runs over, the one named last changes fastest.
Arguments:
- activations: bfloat16 [8, 2, 16384, 4096], P('island', None, 'fsdp'), may hold values from -500 to 500, as said below
- cotangent: bfloat16 [8, 2, 16384, 128], P('island', None, 'fsdp'), may hold values from -6 to 6
- island_params: float32 [8, 4096, 256], P('island', 'fsdp'), may hold values from -6 to 6
- first_moment: float32 [8, 4096, 256], P('island', 'fsdp'), may hold values from -4 to 4
- second_moment: float32 [8, 4096, 256], P('island', 'fsdp'), may hold values from 0.01 to 1
- anchor: float32 [4096, 256], P('fsdp'), may hold values from -6 to 6
- momentum: float32 [4096, 256], P('fsdp'), may hold values from -4 to 4
Outputs:
- new_anchor: float32 [4096, 256], P('fsdp')
- new_momentum: float32 [4096, 256], P('fsdp')
- new_first: float32 [8, 4096, 256], P('island', 'fsdp')
- new_second: float32 [8, 4096, 256], P('island', 'fsdp')
Inputs may be any that keep to these rules, and one draw needn't show every extreme that they name: `activations`: finite layer inputs.
All inputs are finite; a program needn't handle non-finite values.
Results may differ from a plain program's by a relative error of at most 0.0003.
Values sent between devices are 32-bit elements; how exact they have to be, the bound alone decides.
A program may use at most 64 MiB of HBM per device.

v0:
```python
import jax
import jax.numpy as jnp
from jax import lax
from jax.sharding import PartitionSpec as P

D = 4096


def shards(activations, cotangent, island_params, first_moment, second_moment, anchor, momentum):
    row_total = anchor.shape[0]
    inputs_local = activations[0]
    outputs_local = cotangent[0]
    product = jnp.einsum(
        "ltd,lth->dlh", inputs_local, outputs_local, preferred_element_type=jnp.float32
    )
    gradient = lax.psum_scatter(
        product.reshape(lax.axis_size("fsdp") * row_total, -1),
        "fsdp",
        scatter_dimension=0,
        tiled=True,
    )
    squares = lax.psum(jnp.sum(gradient * gradient), "fsdp")
    clip_limit = 0.5 * jnp.sqrt(jnp.float32(D * gradient.shape[1]))
    factor = jnp.minimum(1.0, clip_limit / (jnp.sqrt(squares) + 1e-06))
    clipped = factor * gradient
    new_first = 0.9 * first_moment[0] + 0.1 * clipped
    new_second = 0.95 * second_moment[0] + 0.05 * clipped * clipped
    params_local = island_params[0]
    stepped = params_local - 0.05 * (
        new_first / (jnp.sqrt(new_second) + 1e-08) + 0.1 * params_local
    )
    drift = anchor - stepped
    replicas = lax.axis_size("island")
    mean_drift = lax.psum(drift, "island") / replicas
    new_momentum = 0.9 * momentum + mean_drift
    new_anchor = anchor - 0.7 * (mean_drift + 0.9 * new_momentum)
    return (new_anchor, new_momentum, new_first[None], new_second[None])


def solution(mesh):
    return jax.shard_map(
        shards,
        mesh=mesh,
        in_specs=(
            P("island", None, "fsdp", None),
            P("island", None, "fsdp", None),
            P("island", "fsdp", None),
            P("island", "fsdp", None),
            P("island", "fsdp", None),
            P("fsdp", None),
            P("fsdp", None),
        ),
        out_specs=(
            P("fsdp", None),
            P("fsdp", None),
            P("island", "fsdp", None),
            P("island", "fsdp", None),
        ),
        check_vma=False,
    )
```

profile of v0, /device:TPU:1, one launch (start us, length us, event | category | flops | bytes accessed | tf_op | source)
XLA Modules:
  0.0 466.5 jit_solution(18239322341329438226)
XLA Ops:
  7.2 0.0 copy-start
  7.2 0.0 reduce-scatter.2.cloned.1.call-start
  7.2 0.8 copy-done
  8.1 4.9 %fusion = f32[2,128,4096]{2,1,0:T(8,128)} fusion(bf16[1,2,256,4096]{3,2,1,0:T(8,128)(2,1)} %param.7, bf16[1,2,256,128]{3,2,1,0:T(8,128)(2,1)S(1)} %copy-done), kind=kOutput, calls=%fused_computation | convolution fusion | flops 536870912 | bytes 8519680 | tf_op jit(solution)/shard_map/ltd,lth->dlh/dot_general | solution.py:13
  13.0 5.6 %copy.12 = f32[4096,256]{1,0:T(8,128)} copy(f32[4096,256]{0,1:T(8,128)} %bitcast.36) | data formatting | bytes 8388608 | tf_op jit(solution)/shard_map/reshape | solution.py:17
  18.6 0.0 copy-start.1
  18.6 0.0 copy-start.2
  18.6 0.0 copy-start.3
  18.6 0.0 copy-start.4
  18.6 0.0 copy-start.5
  18.6 0.0 reduce-scatter.2.cloned.1.call-update
  18.7 0.0 all-reduce.2.cloned.1.call-start
  18.7 233.7 %reduce-scatter.2.cloned.1.call-done = f32[64,256]{1,0:T(8,128)} async-done(((f32[4096,256]{1,0:T(8,128)}), f32[64,256]{1,0:T(8,128)}) %reduce-scatter.2.cloned.1.call-update) | async-done | bytes 65552 | tf_op jit(solution)/shard_map/reduce_scatter | solution.py:16
  252.4 1.5 multiply_reduce_fusion
  253.9 109.1 %psum.14 = f32[]{:T(128)} all-reduce(f32[]{:T(128)} %multiply_reduce_fusion), channel_id=1, replica_groups=mesh['island'=8,'fsdp'=64] {'fsdp'}, use_global_device_ids=true, to_apply=%region_2.0 | all-reduce | flops 1 | bytes 8 | tf_op jit(solution)/shard_map/psum | solution.py:22
  363.8 0.0 copy-done.1
  363.8 0.0 copy-done.2
  363.8 0.0 copy-done.3
  363.8 0.0 copy-done.4
  363.8 1.6 fusion.8
  365.4 0.0 all-reduce.2.cloned.1.call-update
  365.4 92.8 %all-reduce.2.cloned.1.call-done = f32[64,256]{1,0:T(8,128)} async-done(((f32[64,256]{1,0:T(8,128)}), f32[64,256]{1,0:T(8,128)}) %all-reduce.2.cloned.1.call-update) | async-done | bytes 65552 | tf_op jit(solution)/shard_map/psum | solution.py:34
  458.2 0.0 copy-done.5
  458.2 1.5 multiply_subtract_fusion
Async XLA Ops:
  7.2 0.9 copy-start
  7.2 245.3 %reduce-scatter.2.cloned.1.call-start = ((), (), s32[]{:S(2)}) async-start(), calls=%async_computation.1 | async-start | bytes 4259840 | tf_op jit(solution)/shard_map/reduce_scatter | solution.py:16
  18.6 345.2 %copy-start.1 = (f32[64,256]{1,0:T(8,128)S(1)}, f32[64,256]{1,0:T(8,128)}, u32[]{:S(2)}) copy-start(f32[64,256]{1,0:T(8,128)} %param.12) | copy-start | bytes 196612
  18.6 345.2 %copy-start.2 = (f32[1,64,256]{2,1,0:T(8,128)S(1)}, f32[1,64,256]{2,1,0:T(8,128)}, u32[]{:S(2)}) copy-start(f32[1,64,256]{2,1,0:T(8,128)} %param.11) | copy-start | bytes 196612
  18.6 345.2 %copy-start.3 = (f32[1,64,256]{2,1,0:T(8,128)S(1)}, f32[1,64,256]{2,1,0:T(8,128)}, u32[]{:S(2)}) copy-start(f32[1,64,256]{2,1,0:T(8,128)} %param.10) | copy-start | bytes 196612
  18.6 345.2 %copy-start.4 = (f32[1,64,256]{2,1,0:T(8,128)S(1)}, f32[1,64,256]{2,1,0:T(8,128)}, u32[]{:S(2)}) copy-start(f32[1,64,256]{2,1,0:T(8,128)} %param.9) | copy-start | bytes 196612
  18.6 439.6 %copy-start.5 = (f32[64,256]{1,0:T(8,128)S(1)}, f32[64,256]{1,0:T(8,128)}, u32[]{:S(2)}) copy-start(f32[64,256]{1,0:T(8,128)} %param.13) | copy-start | bytes 196612
  18.7 439.5 %all-reduce.2.cloned.1.call-start = ((), (), s32[]{:S(2)}) async-start(), calls=%async_computation.2 | async-start | bytes 131072 | tf_op jit(solution)/shard_map/psum | solution.py:34
Sparse Core Ops, SparseCore 0:
  18.8 233.6 reduce-scatter.1
  365.5 92.6 all-reduce.1
where the time goes:
time: 471 us; the launch traced here: 467 us
  waiting for transfers between devices  327 us (69%)
  blocking collectives  109 us (23%)
  between operations  14.8 us (3%)
  local copies, waits for them, and re-layouts  6.49 us (1%)
  matrix products  4.92 us (1%)
    reduce_scatter x1, waiting for transfers between devices, shards(): lax.psum_scatter(product.reshape(lax.axis_size('fsdp') * row_total, -1),...  234 us
    psum x1, blocking collectives, shards(): squares = lax.psum(jnp.sum(gradient * gradient), 'fsdp')  109 us
    psum x1, waiting for transfers between devices, shards(): mean_drift = lax.psum(drift, 'island') / replicas  92.8 us
  transfers between devices with their start and end apart: 2, of which 2 were waited for; matrix products, arithmetic and copies ran while one was open for 0% of the time, Pallas kernels for 0%

commit v1 on v0

v1 whole, which is shorter than its diff:
```python
import functools

import jax
import jax.numpy as jnp
from jax import lax
from jax.experimental import pallas as pl
from jax.experimental.pallas import tpu as pltpu
from jax.sharding import PartitionSpec as P

MESH = pl.DeviceIdType.MESH
F32 = jnp.float32
RX = 104
RC = 128 - RX


def kernel(nz, ni, clip_limit, act, cot, par, fm, sm, anc, o_cl, o_md,
           a_v, c_v, ct, pp, h, pr, xv, ar, al, cr, cl, xz, gt, gs, gb, ssl, dr, drr, md, st, res,
           ld_sem, cs, cr_sem, xs, xr, rs, rr, ms, mr, ss_s, ss_r, is_s, is_r, os):
    half = nz // 2
    i, f = lax.axis_index("island"), lax.axis_index("fsdp")
    z, x, c = f // 4, (f // 2) % 2, f % 2
    ox, oc = 1 - x, 1 - c
    rows = 64 // ni

    def dev(dz=0, xx=None, cc=None):
        zz = lax.rem(z + dz + nz, nz)
        return (i, zz * 4 + (x if xx is None else xx) * 2 + (c if cc is None else cc))

    def copy(src, dst, s, r, to):
        return pltpu.make_async_remote_copy(src_ref=src, dst_ref=dst, send_sem=s, recv_sem=r, device_id=to, device_id_type=MESH)

    barrier = pltpu.get_barrier_semaphore()

    def offset(k):
        return (2 * (k % 2) - 1) * (half - (k + 1) // 2)

    def load(k):
        zk = lax.rem(z + offset(k) + nz, nz)
        return pltpu.make_async_copy(act.at[0, :, :, pl.ds(pl.multiple_of(zk * 256, 256), 256)], a_v.at[k], ld_sem.at[k])

    def at_k(o):
        return 0 if abs(o) == half else 2 * (half - abs(o)) - (1 if o > 0 else 0)

    load_c = pltpu.make_async_copy(cot.at[0], c_v, ld_sem.at[nz])
    load_c.start()
    lax.fori_loop(0, nz, lambda k, _: (load(k).start(), 0)[1], 0)
    state = [pltpu.make_async_copy(src, st.at[n], ld_sem.at[nz + 1 + n])
             for n, src in enumerate((par.at[0], fm.at[0], sm.at[0], anc))]
    for s in state:
        s.start()

    near = [dev(cc=oc), dev(xx=ox), dev(1), dev(-1), dev(2), dev(-2)]
    for to in near:
        pl.semaphore_signal(barrier, inc=1, device_id=to, device_id_type=MESH)

    def greet_islands(n, _):
        pl.semaphore_signal(barrier, inc=1, device_id=(lax.rem(i + n, ni), f), device_id_type=MESH)
        return 0

    lax.fori_loop(1, ni, greet_islands, 0)

    load_c.wait()
    for l in range(2):
        ct[l] = c_v[l].T

    def core_copy(k):
        return copy(pp.at[k], pr.at[k], cs.at[k], cr_sem.at[k], dev(cc=oc))

    def x_copy(k):
        return copy(h.at[k, ox, 0:RX], xv.at[k], xs.at[k], xr.at[k], dev(xx=ox))

    def product(k):
        load(k).wait()
        for l, out in ((oc, pp), (c, h)):
            p = jnp.dot(ct[l], a_v[k, l], preferred_element_type=F32)
            out[k, 0] = p[:, :128]
            out[k, 1] = p[:, 128:]

    def core_sum(k):
        core_copy(k).wait_recv()
        h[k] += pr[k]
        x_copy(k).start()

    product(0)
    pl.semaphore_wait(barrier, len(near) + ni - 1)
    core_copy(0).start()

    streams = {"ar": (0, 1, ar), "al": (1, -1, al), "cr": (2, 1, cr), "cl": (3, -1, cl)}

    def ring(name, o):
        n, sign, buf = streams[name]
        k = at_k(sign * o)
        src = h.at[k, x, 0:RX] if name[0] == "a" else h.at[k, :, RX:128]
        return copy(src, buf.at[o], rs.at[n, o], rr.at[n, o], dev(dz=sign * (2 - o % 2)))

    def a_add(k, name, o):
        longest = half if name in ("ar", "cl") else half - 1
        buf = streams[name][2]
        total = None
        for d in (o + 2, o + 1):
            if d <= longest and (d % 2 or d == o + 2):
                ring(name, d).wait_recv()
                total = buf[d] if total is None else total + buf[d]
        return total

    def chain_a(name, o):
        k = at_k(streams[name][1] * o)
        x_copy(k).wait_recv()
        t = h[k, x, 0:RX] + xv[k]
        if o % 2 == 0 and o < half:
            t = t + a_add(k, name, o)
        h[k, x, 0:RX] = t
        ring(name, o).start()

    def chain_c(name, o):
        if o % 2 == 0 and o < half:
            k = at_k(streams[name][1] * o)
            h[k, :, RX:128] += a_add(k, name, o)
        ring(name, o).start()

    def group(g):
        return [0] if g == 0 else ([nz - 1] if g == half else [2 * g - 1, 2 * g])

    def produce(g):
        for k in group(g):
            product(k)
            core_copy(k).start()

    def collect(g):
        for k in group(g):
            core_sum(k)
        if g == 0:
            chain_c("cl", half)
        elif (half - g) % 2:
            chain_c("cr", half - g)
            chain_c("cl", half - g)

    produce(1)
    collect(0)
    for g in range(2, half + 1):
        produce(g)
        collect(g - 1)
    collect(half)

    chain_a("ar", half)
    for o in range(half - 1, 0, -1):
        if o % 2:
            chain_a("ar", o)
            chain_a("al", o)
        else:
            chain_c("cr", o)
            chain_c("cl", o)
            chain_a("ar", o)
            chain_a("al", o)
        if o == 2:
            last = nz - 1
            h[last, :, RX:128] += a_add(last, "cr", 0) + a_add(last, "cl", 0)
            zx = copy(h.at[last, ox, RX:128], xz, ms.at[0], mr.at[0], dev(xx=ox))
            zx.start()
    x_copy(last).wait_recv()
    gt[0:RX] = h[last, x, 0:RX] + xv[last] + a_add(last, "ar", 0) + a_add(last, "al", 0)
    zx.wait_recv()
    gt[RX:128] = h[last, x, RX:128] + xz[...]

    g = gt[...]
    ssl[0] = jnp.sum(g * g, axis=0, keepdims=True)

    def ss_copy(n):
        return copy(ssl.at[0], ssl.at[n], ss_s.at[n], ss_r.at[n], (i, lax.rem(f + n, 4 * nz)))

    def ss_start(n, _):
        ss_copy(2 * nz + n).start()
        ss_copy(2 * nz - n).start()
        return 0

    ss_copy(2 * nz).start()
    lax.fori_loop(1, 2 * nz, ss_start, 0)

    gt[...] = g.T
    gs[...] = gt[pl.ds(pl.multiple_of(oc * 64, 64), 64)]
    gx = copy(gs, gb.at[c], ms.at[1], mr.at[1], dev(cc=oc))
    gx.start()
    gb[c] = gt[pl.ds(pl.multiple_of(c * 64, 64), 64)]
    for s in state:
        s.wait()
    gx.wait_recv()

    def ss_wait(n, _):
        ss_copy(n).wait_recv()
        return 0

    lax.fori_loop(1, 4 * nz, ss_wait, 0)
    squares = jnp.sum(jnp.sum(ssl[...], axis=0), axis=-1, keepdims=True)
    factor = jnp.minimum(1.0, clip_limit / (jnp.sqrt(squares) + 1e-06))

    for l in range(2):
        col = slice(l * 128, (l + 1) * 128)
        clipped = factor * gb[l]
        nf = 0.9 * st[1, :, col] + 0.1 * clipped
        ns = 0.95 * st[2, :, col] + 0.05 * clipped * clipped
        p = st[0, :, col]
        stepped = p - 0.05 * (nf / (jnp.sqrt(ns) + 1e-08) + 0.1 * p)
        dr[:, col] = st[3, :, col] - stepped
        res[:, col] = clipped

    outs = [pltpu.make_async_copy(src, dst, os.at[n]) for n, (src, dst) in enumerate(((res, o_cl), (md, o_md)))]

    mine = pl.ds(pl.multiple_of(i * rows, rows), rows)

    def to_island(n):
        return (lax.rem(i + n, ni), f)

    def dr_copy(n):
        j = lax.rem(i + n, ni)
        return copy(dr.at[pl.ds(pl.multiple_of(j * rows, rows), rows)], drr.at[n], is_s.at[0, n], is_r.at[0, n], to_island(n))

    def md_copy(n):
        return copy(md.at[mine], md.at[mine], is_s.at[1, n], is_r.at[1, n], to_island(n))

    for n in range(1, ni):
        dr_copy(n).start()
    outs[0].start()
    total = dr[mine]
    for n in range(1, ni):
        dr_copy(n).wait_recv()
        total = total + drr[n]
    md[mine] = total / ni
    for n in range(1, ni):
        md_copy(n).start()
    for n in range(1, ni):
        md_copy(n).wait_recv()
    outs[1].start()

    def sent_k(k, _):
        core_copy(k).wait_send()
        x_copy(k).wait_send()
        return 0

    lax.fori_loop(0, nz, sent_k, 0)
    for name, longest in (("ar", half), ("al", half - 1), ("cr", half - 1), ("cl", half)):
        for o in range(1, longest + 1):
            ring(name, o).wait_send()
    zx.wait_send()
    gx.wait_send()

    def sent_ss(n, _):
        ss_copy(n).wait_send()
        return 0

    lax.fori_loop(1, 4 * nz, sent_ss, 0)
    for n in range(1, ni):
        dr_copy(n).wait_send()
        md_copy(n).wait_send()
    for o in outs:
        o.wait()


def shards(act, cot, par, fm, sm, anc, mom):
    nf, ni = lax.axis_size("fsdp"), lax.axis_size("island")
    nz = nf // 4
    half = nz // 2
    tok = act.shape[2]
    limit = 0.5 * float(act.shape[3] * 256) ** 0.5
    hbm = pl.BlockSpec(memory_space=pl.ANY)
    vm, dma = pltpu.VMEM, pltpu.SemaphoreType.DMA
    clipped, mean_drift = pl.pallas_call(
        functools.partial(kernel, nz, ni, limit),
        out_shape=[jax.ShapeDtypeStruct(anc.shape, F32)] * 2,
        in_specs=[hbm] * 6,
        out_specs=[hbm] * 2,
        scratch_shapes=[
            vm((nz, 2, tok, 256), jnp.bfloat16), vm((2, tok, 128), jnp.bfloat16), vm((2, 128, tok), jnp.bfloat16),
            vm((nz, 2, 128, 128), F32), vm((nz, 2, 128, 128), F32), vm((nz, 2, 128, 128), F32),
            vm((nz, RX, 128), F32),
            vm((half + 1, RX, 128), F32), vm((half + 1, RX, 128), F32),
            vm((half + 1, 2, RC, 128), F32), vm((half + 1, 2, RC, 128), F32),
            vm((RC, 128), F32), vm((128, 128), F32), vm((64, 128), F32), vm((2, 64, 128), F32),
            vm((nf, 1, 128), F32),
            vm((64, 256), F32), vm((ni, 64 // ni, 256), F32), vm((64, 256), F32),
            vm((4, 64, 256), F32), vm((64, 256), F32),
            dma((nz + 5,)), dma((nz,)), dma((nz,)), dma((nz,)), dma((nz,)),
            dma((4, half + 1)), dma((4, half + 1)), dma((2,)), dma((2,)),
            dma((nf,)), dma((nf,)), dma((2, ni)), dma((2, ni)), dma((2,)),
        ],
        compiler_params=pltpu.CompilerParams(collective_id=0, has_side_effects=True, vmem_limit_bytes=62 << 20),
    )(act, cot, par, fm, sm, anc)
    new_first = 0.9 * fm[0] + 0.1 * clipped
    new_second = 0.95 * sm[0] + 0.05 * clipped * clipped
    new_mom = 0.9 * mom + mean_drift
    new_anc = anc - 0.7 * (mean_drift + 0.9 * new_mom)
    return new_anc, new_mom, new_first[None], new_second[None]


def solution(mesh):
    return jax.shard_map(
        shards,
        mesh=mesh,
        in_specs=(
            P("island", None, "fsdp", None),
            P("island", None, "fsdp", None),
            P("island", "fsdp", None),
            P("island", "fsdp", None),
            P("island", "fsdp", None),
            P("fsdp", None),
            P("fsdp", None),
        ),
        out_specs=(
            P("fsdp", None),
            P("fsdp", None),
            P("island", "fsdp", None),
            P("island", "fsdp", None),
        ),
        check_vma=False,
    )
```

time: 471 us -> 69.1 us (0.15)
  waiting for transfers between devices: 327 us -> 0 us
  blocking collectives: 109 us -> 0 us
  Pallas kernels: 0 us -> 64.3 us
  between operations: 14.8 us -> 0.69 us
  local copies, waits for them, and re-layouts: 6.49 us -> 0.02 us
  matrix products: 4.92 us -> 0 us
    reduce_scatter x1 -> x0, waiting for transfers between devices: 234 us -> none  [shards(): lax.psum_scatter(product.reshape(lax.axis_size('fsdp') * row_total, -1),...]
    psum x1 -> x0, blocking collectives: 109 us -> none  [shards(): squares = lax.psum(jnp.sum(gradient * gradient), 'fsdp')]
    psum x1 -> x0, waiting for transfers between devices: 92.8 us -> none  [shards(): mean_drift = lax.psum(drift, 'island') / replicas]
    pallas_call x0 -> x1, Pallas kernels: none -> 64.3 us  [shards(): pl.pallas_call(functools.partial(kernel, nz, ni, limit), out_shape=[jax.S...]
    reshape x1 -> x0, local copies, waits for them, and re-layouts: 5.61 us -> none  [shards(): product.reshape(lax.axis_size('fsdp') * row_total, -1)]
    dot_general x1 -> x0, matrix products: 4.92 us -> none  [shards(): jnp.einsum('ltd,lth->dlh', inputs_local, outputs_local, preferred_element...]
  transfers between devices with their start and end apart: 2 -> 0, of which waited for: 2 -> 0; matrix products, arithmetic and copies ran while one was open for 0% -> 0% of each run, Pallas kernels for 0% -> 0%
where the time goes in v1:
time: 69.1 us; the launch traced here: 68 us
  Pallas kernels  64.3 us (93%)
  other arithmetic  3.02 us (4%)
    pallas_call x1, Pallas kernels, shards(): pl.pallas_call(functools.partial(kernel, nz, ni, limit), out_shape=[jax.S...  64.3 us
    broadcast_in_dim x1, other arithmetic, shards(): return (new_anc, new_mom, new_first[None], new_second[None])  1.51 us
    sub x1, other arithmetic, shards(): new_anc = anc - 0.7 * (mean_drift + 0.9 * new_mom)  1.5 us

profile of v1, /device:TPU:1, one launch (start us, length us, event | category | flops | bytes accessed | tf_op | source)
XLA Modules:
  0.0 68.0 jit_solution(4231602663238463537)
XLA Ops:
  0.6 0.0 copy-start
  0.6 0.0 copy-start.2
  0.7 0.0 copy-start.1
  0.7 0.0 copy-start.3
  0.7 64.3 %shard_map.102 = (f32[64,256]{1,0:T(8,128)}, f32[64,256]{1,0:T(8,128)}) custom-call(bf16[1,2,256,4096]{3,2,1,0:T(8,128)(2,1)} %act.1, bf16[1,2,256,128]{3,2,1,0:T(8,128)(2,1)} %cot.1, f32[1,64,256]{2,1,0:T(8,128)} %par.1, f32[1,64,256]{2,1,0:T(8,128)} %fm.1, f32[1,64,256]{2,1,0:T(8,128)} %sm.1, f32[64,256]{1,0:T(8,128)} %anc.1), custom_call_target="tpu_custom_call" | custom-call | tf_op jit(solution)/shard_map/pallas_call | solution.py:266
  65.0 0.0 copy-done
  65.0 0.0 copy-done.3
  65.0 1.5 %multiply_subtract_fusion = (f32[64,256]{1,0:T(8,128)}, f32[64,256]{1,0:T(8,128)}) fusion(f32[64,256]{1,0:T(8,128)S(1)} %copy-done, f32[64,256]{1,0:T(8,128)} %get-tuple-element.6, f32[64,256]{1,0:T(8,128)S(1)} %copy-done.3), kind=kLoop, calls=%fused_computation.5 | loop fusion | flops 98304 | bytes 327680 | tf_op jit(solution)/shard_map/sub | solution.py:290
  66.5 0.0 copy-done.2
  66.5 0.0 copy-done.1
  66.5 1.5 %fusion.1 = (f32[1,64,256]{2,1,0:T(8,128)}, f32[1,64,256]{2,1,0:T(8,128)}) fusion(f32[64,256]{1,0:T(8,128)} %get-tuple-element.7, f32[1,64,256]{2,1,0:T(8,128)S(1)} %copy-done.2, f32[1,64,256]{2,1,0:T(8,128)S(1)} %copy-done.1), kind=kLoop, calls=%fused_computation.2 | loop fusion | flops 114688 | bytes 327680 | tf_op jit(solution)/shard_map/broadcast_in_dim | solution.py:291
Async XLA Ops:
  0.6 64.4 %copy-start = (f32[64,256]{1,0:T(8,128)S(1)}, f32[64,256]{1,0:T(8,128)}, u32[]{:S(2)}) copy-start(f32[64,256]{1,0:T(8,128)} %anc.1) | copy-start | bytes 196612
  0.6 65.9 %copy-start.2 = (f32[1,64,256]{2,1,0:T(8,128)S(1)}, f32[1,64,256]{2,1,0:T(8,128)}, u32[]{:S(2)}) copy-start(f32[1,64,256]{2,1,0:T(8,128)} %sm.1) | copy-start | bytes 196612
  0.7 65.9 %copy-start.1 = (f32[1,64,256]{2,1,0:T(8,128)S(1)}, f32[1,64,256]{2,1,0:T(8,128)}, u32[]{:S(2)}) copy-start(f32[1,64,256]{2,1,0:T(8,128)} %fm.1) | copy-start | bytes 196612
  0.7 64.3 %copy-start.3 = (f32[64,256]{1,0:T(8,128)S(1)}, f32[64,256]{1,0:T(8,128)}, u32[]{:S(2)}) copy-start(f32[64,256]{1,0:T(8,128)} %param.13) | copy-start | bytes 196612

commit v2 on v1

--- a/solution.py
+++ b/solution.py
@@ -9,13 +9,15 @@
 
 MESH = pl.DeviceIdType.MESH
 F32 = jnp.float32
-RX = 104
+STREAMS = ((0, 56, True, 1), (56, 112, True, -1), (112, 128, False, -1))
+PRE, LAG, PA, PB, PC = 2, 3, 4, 6, 7
+RX = 112
 RC = 128 - RX
 
 
 def kernel(nz, ni, clip_limit, act, cot, par, fm, sm, anc, o_cl, o_md,
-           a_v, c_v, ct, pp, h, pr, xv, ar, al, cr, cl, xz, gt, gs, gb, ssl, dr, drr, md, st, res,
-           ld_sem, cs, cr_sem, xs, xr, rs, rr, ms, mr, ss_s, ss_r, is_s, is_r, os):
+           a_v, c_v, ct, pp, h, pr, xv, ring_a, ring_c, xz, gt, gs, gb, ssl, dr, drr, md, st, res,
+           word, ld_sem, cs, cr_sem, xs, xr, rs, rr, ms, mr, ss_s, ss_r, is_s, is_r, os):
     half = nz // 2
     i, f = lax.axis_index("island"), lax.axis_index("fsdp")
     z, x, c = f // 4, (f // 2) % 2, f % 2
@@ -49,25 +51,37 @@
     for s in state:
         s.start()
 
-    near = [dev(cc=oc), dev(xx=ox), dev(1), dev(-1), dev(2), dev(-2)]
-    for to in near:
+    yy, xp = i // 2, 2 * lax.rem(i, 2) + x
+
+    def beside(dy, dx, dz):
+        xq = lax.rem(xp + dx + 4, 4)
+        return (lax.rem(yy + dy + ni // 2, ni // 2) * 2 + xq // 2, lax.rem(z + dz + nz, nz) * 4 + lax.rem(xq, 2) * 2 + c)
+
+    sides = [beside(1, 0, 0), beside(-1, 0, 0), beside(0, 1, 0), beside(0, -1, 0), beside(0, 0, 1), beside(0, 0, -1)]
+    for to in sides + [dev(cc=oc)]:
         pl.semaphore_signal(barrier, inc=1, device_id=to, device_id_type=MESH)
 
-    def greet_islands(n, _):
-        pl.semaphore_signal(barrier, inc=1, device_id=(lax.rem(i + n, ni), f), device_id_type=MESH)
-        return 0
-
-    lax.fori_loop(1, ni, greet_islands, 0)
+    def tell(r, which):
+        for d in which:
+            pl.semaphore_signal(word.at[r, d], inc=1, device_id=sides[d], device_id_type=MESH)
+
+    def hear(r, which):
+        for d in which:
+            pl.semaphore_wait(word.at[r, d], 1)
 
     load_c.wait()
     for l in range(2):
         ct[l] = c_v[l].T
 
+    first_x = [n for n, t in enumerate(STREAMS) if t[2]]
+    last_x = [n for n, t in enumerate(STREAMS) if not t[2]]
+
     def core_copy(k):
         return copy(pp.at[k], pr.at[k], cs.at[k], cr_sem.at[k], dev(cc=oc))
 
-    def x_copy(k):
-        return copy(h.at[k, ox, 0:RX], xv.at[k], xs.at[k], xr.at[k], dev(xx=ox))
+    def x_copy(k, n):
+        lo, hi = STREAMS[n][:2]
+        return copy(h.at[k, ox, lo:hi], xv.at[k, lo:hi], xs.at[n, k], xr.at[n, k], dev(xx=ox))
 
     def product(k):
         load(k).wait()
@@ -79,87 +93,113 @@
     def core_sum(k):
         core_copy(k).wait_recv()
         h[k] += pr[k]
-        x_copy(k).start()
-
-    product(0)
-    pl.semaphore_wait(barrier, len(near) + ni - 1)
-    core_copy(0).start()
-
-    streams = {"ar": (0, 1, ar), "al": (1, -1, al), "cr": (2, 1, cr), "cl": (3, -1, cl)}
-
-    def ring(name, o):
-        n, sign, buf = streams[name]
+        for n in first_x:
+            x_copy(k, n).start()
+
+    early = 2 * PRE + 1
+    for k in range(early):
+        product(k)
+    pl.semaphore_wait(barrier, len(sides) + 1)
+    tell(0, range(6))
+    for k in range(early):
+        core_copy(k).start()
+
+    def longest(n, sign):
+        return half if sign == STREAMS[n][3] else half - 1
+
+    def landed(n, sign, o):
+        lo, hi, first, _ = STREAMS[n]
+        d = (sign + 1) // 2
+        return ring_a.at[d, o, lo:hi] if first else ring_c.at[d, o, :, lo - RX:hi - RX]
+
+    def ring(n, sign, o):
+        lo, hi, first, _ = STREAMS[n]
         k = at_k(sign * o)
-        src = h.at[k, x, 0:RX] if name[0] == "a" else h.at[k, :, RX:128]
-        return copy(src, buf.at[o], rs.at[n, o], rr.at[n, o], dev(dz=sign * (2 - o % 2)))
-
-    def a_add(k, name, o):
-        longest = half if name in ("ar", "cl") else half - 1
-        buf = streams[name][2]
+        d = (sign + 1) // 2
+        src = h.at[k, x, lo:hi] if first else h.at[k, :, lo:hi]
+        return copy(src, landed(n, sign, o), rs.at[n, d, o], rr.at[n, d, o], dev(dz=sign * (2 - o % 2)))
+
+    def come(n, sign, o):
         total = None
         for d in (o + 2, o + 1):
-            if d <= longest and (d % 2 or d == o + 2):
-                ring(name, d).wait_recv()
-                total = buf[d] if total is None else total + buf[d]
+            if d <= longest(n, sign):
+                ring(n, sign, d).wait_recv()
+                part = landed(n, sign, d)[...]
+                total = part if total is None else total + part
         return total
 
-    def chain_a(name, o):
-        k = at_k(streams[name][1] * o)
-        x_copy(k).wait_recv()
-        t = h[k, x, 0:RX] + xv[k]
-        if o % 2 == 0 and o < half:
-            t = t + a_add(k, name, o)
-        h[k, x, 0:RX] = t
-        ring(name, o).start()
-
-    def chain_c(name, o):
-        if o % 2 == 0 and o < half:
-            k = at_k(streams[name][1] * o)
-            h[k, :, RX:128] += a_add(k, name, o)
-        ring(name, o).start()
+    def pass_on(n, sign, o):
+        lo, hi, first, _ = STREAMS[n]
+        if o > longest(n, sign):
+            return
+        k = at_k(sign * o)
+        t = come(n, sign, o) if o % 2 == 0 else None
+        if first:
+            x_copy(k, n).wait_recv()
+            own = h[k, x, lo:hi] + xv[k, lo:hi]
+            h[k, x, lo:hi] = own if t is None else own + t
+        elif t is not None:
+            h[k, :, lo:hi] += t
+        ring(n, sign, o).start()
+
+    def pass_all(which, o):
+        for n in which:
+            for sign in (1, -1):
+                pass_on(n, sign, o)
 
     def group(g):
         return [0] if g == 0 else ([nz - 1] if g == half else [2 * g - 1, 2 * g])
 
     def produce(g):
         for k in group(g):
-            product(k)
-            core_copy(k).start()
+            if k >= early:
+                product(k)
+                core_copy(k).start()
 
     def collect(g):
         for k in group(g):
             core_sum(k)
         if g == 0:
-            chain_c("cl", half)
-        elif (half - g) % 2:
-            chain_c("cr", half - g)
-            chain_c("cl", half - g)
-
-    produce(1)
-    collect(0)
-    for g in range(2, half + 1):
+            hear(0, (4, 5))
+        if g == 0 or (half - g) % 2:
+            pass_all(last_x, half - g)
+
+    for g in range(1, LAG + 1):
         produce(g)
-        collect(g - 1)
-    collect(half)
-
-    chain_a("ar", half)
-    for o in range(half - 1, 0, -1):
-        if o % 2:
-            chain_a("ar", o)
-            chain_a("al", o)
-        else:
-            chain_c("cr", o)
-            chain_c("cl", o)
-            chain_a("ar", o)
-            chain_a("al", o)
+    for g in range(half + 1):
+        collect(g)
+        if g + LAG < half:
+            produce(g + LAG + 1)
+        if g == PA:
+            pass_all(first_x, half)
+        if g == PC:
+            pass_all(last_x, half - 2)
+        if g == PB:
+            pass_all(first_x, half - 1)
+
+    hear(0, range(4))
+    tell(1, range(4))
+    last = nz - 1
+    zx = [copy(h.at[last, ox, STREAMS[n][0]:STREAMS[n][1]], xz.at[STREAMS[n][0] - RX:STREAMS[n][1] - RX],
+               ms.at[2 + n], mr.at[2 + n], dev(xx=ox)) for n in last_x]
+    for o in range(half - 2, 0, -1):
+        if o == half // 2:
+            hear(1, range(4))
+            tell(2, range(4))
+        if o % 2 == 0 and o < half - 2:
+            pass_all(last_x, o)
+        pass_all(first_x, o)
         if o == 2:
-            last = nz - 1
-            h[last, :, RX:128] += a_add(last, "cr", 0) + a_add(last, "cl", 0)
-            zx = copy(h.at[last, ox, RX:128], xz, ms.at[0], mr.at[0], dev(xx=ox))
-            zx.start()
-    x_copy(last).wait_recv()
-    gt[0:RX] = h[last, x, 0:RX] + xv[last] + a_add(last, "ar", 0) + a_add(last, "al", 0)
-    zx.wait_recv()
+            for j, n in enumerate(last_x):
+                lo, hi = STREAMS[n][:2]
+                h[last, :, lo:hi] += come(n, 1, 0) + come(n, -1, 0)
+                zx[j].start()
+    for n in first_x:
+        lo, hi = STREAMS[n][:2]
+        x_copy(last, n).wait_recv()
+        gt[lo:hi] = h[last, x, lo:hi] + xv[last, lo:hi] + come(n, 1, 0) + come(n, -1, 0)
+    for c_x in zx:
+        c_x.wait_recv()
     gt[RX:128] = h[last, x, RX:128] + xz[...]
 
     g = gt[...]
@@ -176,6 +216,7 @@
     ss_copy(2 * nz).start()
     lax.fori_loop(1, 2 * nz, ss_start, 0)
 
+    hear(2, range(4))
     gt[...] = g.T
     gs[...] = gt[pl.ds(pl.multiple_of(oc * 64, 64), 64)]
     gx = copy(gs, gb.at[c], ms.at[1], mr.at[1], dev(cc=oc))
@@ -233,14 +274,17 @@
 
     def sent_k(k, _):
         core_copy(k).wait_send()
-        x_copy(k).wait_send()
+        for n in first_x:
+            x_copy(k, n).wait_send()
         return 0
 
     lax.fori_loop(0, nz, sent_k, 0)
-    for name, longest in (("ar", half), ("al", half - 1), ("cr", half - 1), ("cl", half)):
-        for o in range(1, longest + 1):
-            ring(name, o).wait_send()
-    zx.wait_send()
+    for n in range(len(STREAMS)):
+        for sign in (1, -1):
+            for o in range(1, longest(n, sign) + 1):
+                ring(n, sign, o).wait_send()
+    for c_x in zx:
+        c_x.wait_send()
     gx.wait_send()
 
     def sent_ss(n, _):
@@ -262,6 +306,7 @@
     tok = act.shape[2]
     limit = 0.5 * float(act.shape[3] * 256) ** 0.5
     hbm = pl.BlockSpec(memory_space=pl.ANY)
+    ns = len(STREAMS)
     vm, dma = pltpu.VMEM, pltpu.SemaphoreType.DMA
     clipped, mean_drift = pl.pallas_call(
         functools.partial(kernel, nz, ni, limit),
@@ -272,17 +317,16 @@
             vm((nz, 2, tok, 256), jnp.bfloat16), vm((2, tok, 128), jnp.bfloat16), vm((2, 128, tok), jnp.bfloat16),
             vm((nz, 2, 128, 128), F32), vm((nz, 2, 128, 128), F32), vm((nz, 2, 128, 128), F32),
             vm((nz, RX, 128), F32),
-            vm((half + 1, RX, 128), F32), vm((half + 1, RX, 128), F32),
-            vm((half + 1, 2, RC, 128), F32), vm((half + 1, 2, RC, 128), F32),
+            vm((2, half + 1, RX, 128), F32), vm((2, half + 1, 2, RC, 128), F32),
             vm((RC, 128), F32), vm((128, 128), F32), vm((64, 128), F32), vm((2, 64, 128), F32),
             vm((nf, 1, 128), F32),
             vm((64, 256), F32), vm((ni, 64 // ni, 256), F32), vm((64, 256), F32),
             vm((4, 64, 256), F32), vm((64, 256), F32),
-            dma((nz + 5,)), dma((nz,)), dma((nz,)), dma((nz,)), dma((nz,)),
-            dma((4, half + 1)), dma((4, half + 1)), dma((2,)), dma((2,)),
+            pltpu.SemaphoreType.REGULAR((3, 6)), dma((nz + 5,)), dma((nz,)), dma((nz,)), dma((ns, nz)), dma((ns, nz)),
+            dma((ns, 2, half + 1)), dma((ns, 2, half + 1)), dma((2 + ns,)), dma((2 + ns,)),
             dma((nf,)), dma((nf,)), dma((2, ni)), dma((2, ni)), dma((2,)),
         ],
-        compiler_params=pltpu.CompilerParams(collective_id=0, has_side_effects=True, vmem_limit_bytes=62 << 20),
+        compiler_params=pltpu.CompilerParams(collective_id=0, has_side_effects=True, vmem_limit_bytes=55091 << 10),
     )(act, cot, par, fm, sm, anc)
     new_first = 0.9 * fm[0] + 0.1 * clipped
     new_second = 0.95 * sm[0] + 0.05 * clipped * clipped

time: 69.1 us -> 62.4 us (0.903); the launches traced: 68 us -> 62.2 us
  Pallas kernels: 64.3 us -> 60.2 us
  other arithmetic: 3.02 us -> 1.34 us
    pallas_call x1, Pallas kernels: 64.3 us -> 60.2 us  [shards(): pl.pallas_call(functools.partial(kernel, nz, ni, limit), out_shape=[jax.S...]
    broadcast_in_dim x1, other arithmetic: 1.51 us -> 0.67 us  [shards(): return (new_anc, new_mom, new_first[None], new_second[None])]
    sub x1, other arithmetic: 1.5 us -> 0.67 us  [shards(): new_anc = anc - 0.7 * (mean_drift + 0.9 * new_mom)]
where the time goes in v2:
time: 62.4 us; the launch traced here: 62.2 us
  Pallas kernels  60.2 us (96%)
  other arithmetic  1.34 us (2%)
  between operations  0.69 us (1%)
    pallas_call x1, Pallas kernels, shards(): pl.pallas_call(functools.partial(kernel, nz, ni, limit), out_shape=[jax.S...  60.2 us

profile of v2, /device:TPU:1, one launch (start us, length us, event | category | flops | bytes accessed | tf_op | source)
XLA Modules:
  0.0 62.2 jit_solution(16502064503794506130)
XLA Ops:
  0.6 0.0 copy-start
  0.6 0.0 copy-start.2
  0.7 0.0 copy-start.1
  0.7 0.0 copy-start.3
  0.7 60.2 %shard_map.102 = (f32[64,256]{1,0:T(8,128)S(1)}, f32[64,256]{1,0:T(8,128)S(1)}) custom-call(bf16[1,2,256,4096]{3,2,1,0:T(8,128)(2,1)} %act.1, bf16[1,2,256,128]{3,2,1,0:T(8,128)(2,1)} %cot.1, f32[1,64,256]{2,1,0:T(8,128)} %par.1, f32[1,64,256]{2,1,0:T(8,128)} %fm.1, f32[1,64,256]{2,1,0:T(8,128)} %sm.1, f32[64,256]{1,0:T(8,128)} %anc.1), custom_call_target="tpu_custom_call" | custom-call | tf_op jit(solution)/shard_map/pallas_call | solution.py:311
  60.9 0.0 copy-done
  60.9 0.0 copy-done.3
  60.9 0.7 %multiply_subtract_fusion = (f32[64,256]{1,0:T(8,128)}, f32[64,256]{1,0:T(8,128)}) fusion(f32[64,256]{1,0:T(8,128)S(1)} %copy-done, f32[64,256]{1,0:T(8,128)S(1)} %get-tuple-element.6, f32[64,256]{1,0:T(8,128)S(1)} %copy-done.3), kind=kLoop, calls=%fused_computation.5 | loop fusion | flops 98304 | bytes 327680 | tf_op jit(solution)/shard_map/sub | solution.py:334
  61.6 0.0 copy-done.2
  61.6 0.0 copy-done.1
  61.6 0.7 %fusion.1 = (f32[1,64,256]{2,1,0:T(8,128)}, f32[1,64,256]{2,1,0:T(8,128)}) fusion(f32[64,256]{1,0:T(8,128)S(1)} %get-tuple-element.7, f32[1,64,256]{2,1,0:T(8,128)S(1)} %copy-done.2, f32[1,64,256]{2,1,0:T(8,128)S(1)} %copy-done.1), kind=kLoop, calls=%fused_computation.2 | loop fusion | flops 114688 | bytes 327680 | tf_op jit(solution)/shard_map/broadcast_in_dim | solution.py:335
Async XLA Ops:
  0.6 60.2 %copy-start = (f32[64,256]{1,0:T(8,128)S(1)}, f32[64,256]{1,0:T(8,128)}, u32[]{:S(2)}) copy-start(f32[64,256]{1,0:T(8,128)} %anc.1) | copy-start | bytes 196612
  0.6 60.9 %copy-start.2 = (f32[1,64,256]{2,1,0:T(8,128)S(1)}, f32[1,64,256]{2,1,0:T(8,128)}, u32[]{:S(2)}) copy-start(f32[1,64,256]{2,1,0:T(8,128)} %sm.1) | copy-start | bytes 196612
  0.7 60.9 %copy-start.1 = (f32[1,64,256]{2,1,0:T(8,128)S(1)}, f32[1,64,256]{2,1,0:T(8,128)}, u32[]{:S(2)}) copy-start(f32[1,64,256]{2,1,0:T(8,128)} %fm.1) | copy-start | bytes 196612
  0.7 60.2 %copy-start.3 = (f32[64,256]{1,0:T(8,128)S(1)}, f32[64,256]{1,0:T(8,128)}, u32[]{:S(2)}) copy-start(f32[64,256]{1,0:T(8,128)} %param.13) | copy-start | bytes 196612

commit v3 on v2

--- a/solution.py
+++ b/solution.py
@@ -10,7 +10,7 @@
 MESH = pl.DeviceIdType.MESH
 F32 = jnp.float32
 STREAMS = ((0, 56, True, 1), (56, 112, True, -1), (112, 128, False, -1))
-PRE, LAG, PA, PB, PC = 2, 3, 4, 6, 7
+PRE, LAG, PZ, PA, PB, PC = 1, 4, 3, 4, 6, 7
 RX = 112
 RC = 128 - RX
 
@@ -22,7 +22,7 @@
     i, f = lax.axis_index("island"), lax.axis_index("fsdp")
     z, x, c = f // 4, (f // 2) % 2, f % 2
     ox, oc = 1 - x, 1 - c
-    rows = 64 // ni
+    rows = 128 // ni
 
     def dev(dz=0, xx=None, cc=None):
         zz = lax.rem(z + dz + nz, nz)
@@ -159,9 +159,7 @@
     def collect(g):
         for k in group(g):
             core_sum(k)
-        if g == 0:
-            hear(0, (4, 5))
-        if g == 0 or (half - g) % 2:
+        if (half - g) % 2:
             pass_all(last_x, half - g)
 
     for g in range(1, LAG + 1):
@@ -170,6 +168,9 @@
         collect(g)
         if g + LAG < half:
             produce(g + LAG + 1)
+        if g == PZ:
+            hear(0, (4, 5))
+            pass_all(last_x, half)
         if g == PA:
             pass_all(first_x, half)
         if g == PC:
@@ -206,7 +207,7 @@
     ssl[0] = jnp.sum(g * g, axis=0, keepdims=True)
 
     def ss_copy(n):
-        return copy(ssl.at[0], ssl.at[n], ss_s.at[n], ss_r.at[n], (i, lax.rem(f + n, 4 * nz)))
+        return copy(ssl.at[0], ssl.at[n], ss_s.at[0], ss_r.at[0], (i, lax.rem(f + n, 4 * nz)))
 
     def ss_start(n, _):
         ss_copy(2 * nz + n).start()
@@ -224,13 +225,25 @@
     gb[c] = gt[pl.ds(pl.multiple_of(c * 64, 64), 64)]
     for s in state:
         s.wait()
+
+    def sent_k(k, _):
+        core_copy(k).wait_send()
+        for n in first_x:
+            x_copy(k, n).wait_send()
+        return 0
+
+    lax.fori_loop(0, nz, sent_k, 0)
+    for n in range(len(STREAMS)):
+        for sign in (1, -1):
+            for o in range(1, longest(n, sign) + 1):
+                ring(n, sign, o).wait_send()
+    for c_x in zx:
+        c_x.wait_send()
     gx.wait_recv()
-
-    def ss_wait(n, _):
-        ss_copy(n).wait_recv()
-        return 0
-
-    lax.fori_loop(1, 4 * nz, ss_wait, 0)
+    gx.wait_send()
+
+    all_ss = copy(ssl.at[1:4 * nz], ssl.at[1:4 * nz], ss_s.at[0], ss_r.at[0], dev(cc=oc))
+    all_ss.wait_recv()
     squares = jnp.sum(jnp.sum(ssl[...], axis=0), axis=-1, keepdims=True)
     factor = jnp.minimum(1.0, clip_limit / (jnp.sqrt(squares) + 1e-06))
 
@@ -246,54 +259,40 @@
 
     outs = [pltpu.make_async_copy(src, dst, os.at[n]) for n, (src, dst) in enumerate(((res, o_cl), (md, o_md)))]
 
-    mine = pl.ds(pl.multiple_of(i * rows, rows), rows)
+    mine = pl.ds(pl.multiple_of(yy * rows, rows), rows)
 
     def to_island(n):
         return (lax.rem(i + n, ni), f)
 
     def dr_copy(n):
         j = lax.rem(i + n, ni)
-        return copy(dr.at[pl.ds(pl.multiple_of(j * rows, rows), rows)], drr.at[n], is_s.at[0, n], is_r.at[0, n], to_island(n))
+        return copy(dr.at[pl.ds(pl.multiple_of(j // 2 * rows, rows), rows)], drr.at[i], is_s.at[0, n], is_r.at[0, n], to_island(n))
 
     def md_copy(n):
         return copy(md.at[mine], md.at[mine], is_s.at[1, n], is_r.at[1, n], to_island(n))
 
-    for n in range(1, ni):
+    far = sorted(range(1, ni), key=lambda n: abs(n - ni // 2))
+    for n in far:
         dr_copy(n).start()
     outs[0].start()
-    total = dr[mine]
+    all_ss.wait_send()
+    drr[i] = dr[mine]
+    for n in far:
+        dr_copy(n).wait_recv()
+    total = drr[0]
     for n in range(1, ni):
-        dr_copy(n).wait_recv()
         total = total + drr[n]
     md[mine] = total / ni
-    for n in range(1, ni):
+    back = [n for n in far if n % 2 == 0]
+    for n in back:
         md_copy(n).start()
-    for n in range(1, ni):
+    for n in back:
         md_copy(n).wait_recv()
     outs[1].start()
 
-    def sent_k(k, _):
-        core_copy(k).wait_send()
-        for n in first_x:
-            x_copy(k, n).wait_send()
-        return 0
-
-    lax.fori_loop(0, nz, sent_k, 0)
-    for n in range(len(STREAMS)):
-        for sign in (1, -1):
-            for o in range(1, longest(n, sign) + 1):
-                ring(n, sign, o).wait_send()
-    for c_x in zx:
-        c_x.wait_send()
-    gx.wait_send()
-
-    def sent_ss(n, _):
-        ss_copy(n).wait_send()
-        return 0
-
-    lax.fori_loop(1, 4 * nz, sent_ss, 0)
-    for n in range(1, ni):
+    for n in far:
         dr_copy(n).wait_send()
+    for n in back:
         md_copy(n).wait_send()
     for o in outs:
         o.wait()
@@ -320,11 +319,11 @@
             vm((2, half + 1, RX, 128), F32), vm((2, half + 1, 2, RC, 128), F32),
             vm((RC, 128), F32), vm((128, 128), F32), vm((64, 128), F32), vm((2, 64, 128), F32),
             vm((nf, 1, 128), F32),
-            vm((64, 256), F32), vm((ni, 64 // ni, 256), F32), vm((64, 256), F32),
+            vm((64, 256), F32), vm((ni, 128 // ni, 256), F32), vm((64, 256), F32),
             vm((4, 64, 256), F32), vm((64, 256), F32),
             pltpu.SemaphoreType.REGULAR((3, 6)), dma((nz + 5,)), dma((nz,)), dma((nz,)), dma((ns, nz)), dma((ns, nz)),
             dma((ns, 2, half + 1)), dma((ns, 2, half + 1)), dma((2 + ns,)), dma((2 + ns,)),
-            dma((nf,)), dma((nf,)), dma((2, ni)), dma((2, ni)), dma((2,)),
+            dma((1,)), dma((1,)), dma((2, ni)), dma((2, ni)), dma((2,)),
         ],
         compiler_params=pltpu.CompilerParams(collective_id=0, has_side_effects=True, vmem_limit_bytes=55091 << 10),
     )(act, cot, par, fm, sm, anc)

time: 62.4 us -> 59.4 us (0.952)
  Pallas kernels: 60.2 us -> 57.1 us
    pallas_call x1, Pallas kernels: 60.2 us -> 57.1 us  [shards(): pl.pallas_call(functools.partial(kernel, nz, ni, limit), out_shape=[jax.S...]
where the time goes in v3:
time: 59.4 us; the launch traced here: 59.1 us
  Pallas kernels  57.1 us (96%)
  other arithmetic  1.34 us (2%)
  between operations  0.69 us (1%)
    pallas_call x1, Pallas kernels, shards(): pl.pallas_call(functools.partial(kernel, nz, ni, limit), out_shape=[jax.S...  57.1 us

profile of v3, /device:TPU:1, one launch (start us, length us, event | category | flops | bytes accessed | tf_op | source)
XLA Modules:
  0.0 59.1 jit_solution(2759432760751660545)
XLA Ops:
  0.6 0.0 copy-start
  0.6 0.0 copy-start.2
  0.7 0.0 copy-start.1
  0.7 0.0 copy-start.3
  0.7 57.1 %shard_map.102 = (f32[64,256]{1,0:T(8,128)S(1)}, f32[64,256]{1,0:T(8,128)S(1)}) custom-call(bf16[1,2,256,4096]{3,2,1,0:T(8,128)(2,1)} %act.1, bf16[1,2,256,128]{3,2,1,0:T(8,128)(2,1)} %cot.1, f32[1,64,256]{2,1,0:T(8,128)} %par.1, f32[1,64,256]{2,1,0:T(8,128)} %fm.1, f32[1,64,256]{2,1,0:T(8,128)} %sm.1, f32[64,256]{1,0:T(8,128)} %anc.1), custom_call_target="tpu_custom_call" | custom-call | tf_op jit(solution)/shard_map/pallas_call | solution.py:310
  57.8 0.0 copy-done
  57.8 0.0 copy-done.3
  57.8 0.7 %multiply_subtract_fusion = (f32[64,256]{1,0:T(8,128)}, f32[64,256]{1,0:T(8,128)}) fusion(f32[64,256]{1,0:T(8,128)S(1)} %copy-done, f32[64,256]{1,0:T(8,128)S(1)} %get-tuple-element.6, f32[64,256]{1,0:T(8,128)S(1)} %copy-done.3), kind=kLoop, calls=%fused_computation.5 | loop fusion | flops 98304 | bytes 327680 | tf_op jit(solution)/shard_map/sub | solution.py:333
  58.5 0.0 copy-done.2
  58.5 0.0 copy-done.1
  58.5 0.7 %fusion.1 = (f32[1,64,256]{2,1,0:T(8,128)}, f32[1,64,256]{2,1,0:T(8,128)}) fusion(f32[64,256]{1,0:T(8,128)S(1)} %get-tuple-element.7, f32[1,64,256]{2,1,0:T(8,128)S(1)} %copy-done.2, f32[1,64,256]{2,1,0:T(8,128)S(1)} %copy-done.1), kind=kLoop, calls=%fused_computation.2 | loop fusion | flops 114688 | bytes 327680 | tf_op jit(solution)/shard_map/broadcast_in_dim | solution.py:334
Async XLA Ops:
  0.6 57.2 %copy-start = (f32[64,256]{1,0:T(8,128)S(1)}, f32[64,256]{1,0:T(8,128)}, u32[]{:S(2)}) copy-start(f32[64,256]{1,0:T(8,128)} %anc.1) | copy-start | bytes 196612
  0.6 57.8 %copy-start.2 = (f32[1,64,256]{2,1,0:T(8,128)S(1)}, f32[1,64,256]{2,1,0:T(8,128)}, u32[]{:S(2)}) copy-start(f32[1,64,256]{2,1,0:T(8,128)} %sm.1) | copy-start | bytes 196612
  0.7 57.8 %copy-start.1 = (f32[1,64,256]{2,1,0:T(8,128)S(1)}, f32[1,64,256]{2,1,0:T(8,128)}, u32[]{:S(2)}) copy-start(f32[1,64,256]{2,1,0:T(8,128)} %fm.1) | copy-start | bytes 196612
  0.7 57.1 %copy-start.3 = (f32[64,256]{1,0:T(8,128)S(1)}, f32[64,256]{1,0:T(8,128)}, u32[]{:S(2)}) copy-start(f32[64,256]{1,0:T(8,128)} %param.13) | copy-start | bytes 196612

commit v4 on v3

--- a/solution.py
+++ b/solution.py
@@ -9,9 +9,9 @@
 
 MESH = pl.DeviceIdType.MESH
 F32 = jnp.float32
-STREAMS = ((0, 56, True, 1), (56, 112, True, -1), (112, 128, False, -1))
+STREAMS = ((0, 56, True, 1), (56, 104, True, -1), (104, 128, False, -1))
 PRE, LAG, PZ, PA, PB, PC = 1, 4, 3, 4, 6, 7
-RX = 112
+RX = 104
 RC = 128 - RX
 
 
@@ -44,13 +44,6 @@
         return 0 if abs(o) == half else 2 * (half - abs(o)) - (1 if o > 0 else 0)
 
     load_c = pltpu.make_async_copy(cot.at[0], c_v, ld_sem.at[nz])
-    load_c.start()
-    lax.fori_loop(0, nz, lambda k, _: (load(k).start(), 0)[1], 0)
-    state = [pltpu.make_async_copy(src, st.at[n], ld_sem.at[nz + 1 + n])
-             for n, src in enumerate((par.at[0], fm.at[0], sm.at[0], anc))]
-    for s in state:
-        s.start()
-
     yy, xp = i // 2, 2 * lax.rem(i, 2) + x
 
     def beside(dy, dx, dz):
@@ -61,6 +54,8 @@
     for to in sides + [dev(cc=oc)]:
         pl.semaphore_signal(barrier, inc=1, device_id=to, device_id_type=MESH)
 
+    load_c.start()
+    lax.fori_loop(0, nz, lambda k, _: (load(k).start(), 0)[1], 0)
     def tell(r, which):
         for d in which:
             pl.semaphore_signal(word.at[r, d], inc=1, device_id=sides[d], device_id_type=MESH)
@@ -178,6 +173,10 @@
         if g == PB:
             pass_all(first_x, half - 1)
 
+    state = [pltpu.make_async_copy(src, st.at[n], ld_sem.at[nz + 1 + n])
+             for n, src in enumerate((par.at[0], fm.at[0], sm.at[0], anc))]
+    for s in state:
+        s.start()
     hear(0, range(4))
     tell(1, range(4))
     last = nz - 1
@@ -190,7 +189,7 @@
         if o % 2 == 0 and o < half - 2:
             pass_all(last_x, o)
         pass_all(first_x, o)
-        if o == 2:
+        if o == 1:
             for j, n in enumerate(last_x):
                 lo, hi = STREAMS[n][:2]
                 h[last, :, lo:hi] += come(n, 1, 0) + come(n, -1, 0)

time: 59.4 us -> 58.7 us (0.988)
  Pallas kernels: 57.1 us -> 56.5 us
where the time goes in v4:
time: 58.7 us; the launch traced here: 58.6 us
  Pallas kernels  56.5 us (96%)
  other arithmetic  1.34 us (2%)
  between operations  0.69 us (1%)
    pallas_call x1, Pallas kernels, shards(): pl.pallas_call(functools.partial(kernel, nz, ni, limit), out_shape=[jax.S...  56.5 us

profile of v4, /device:TPU:1, one launch (start us, length us, event | category | flops | bytes accessed | tf_op | source)
XLA Modules:
  0.0 58.6 jit_solution(14845363951818398493)
XLA Ops:
  0.6 0.0 copy-start
  0.6 0.0 copy-start.2
  0.7 0.0 copy-start.1
  0.7 0.0 copy-start.3
  0.7 56.5 %shard_map.102 = (f32[64,256]{1,0:T(8,128)S(1)}, f32[64,256]{1,0:T(8,128)S(1)}) custom-call(bf16[1,2,256,4096]{3,2,1,0:T(8,128)(2,1)} %act.1, bf16[1,2,256,128]{3,2,1,0:T(8,128)(2,1)} %cot.1, f32[1,64,256]{2,1,0:T(8,128)} %par.1, f32[1,64,256]{2,1,0:T(8,128)} %fm.1, f32[1,64,256]{2,1,0:T(8,128)} %sm.1, f32[64,256]{1,0:T(8,128)} %anc.1), custom_call_target="tpu_custom_call" | custom-call | tf_op jit(solution)/shard_map/pallas_call | solution.py:309
  57.2 0.0 copy-done
  57.2 0.0 copy-done.3
  57.2 0.7 %multiply_subtract_fusion = (f32[64,256]{1,0:T(8,128)}, f32[64,256]{1,0:T(8,128)}) fusion(f32[64,256]{1,0:T(8,128)S(1)} %copy-done, f32[64,256]{1,0:T(8,128)S(1)} %get-tuple-element.6, f32[64,256]{1,0:T(8,128)S(1)} %copy-done.3), kind=kLoop, calls=%fused_computation.5 | loop fusion | flops 98304 | bytes 327680 | tf_op jit(solution)/shard_map/sub | solution.py:332
  57.9 0.0 copy-done.2
  57.9 0.0 copy-done.1
  57.9 0.7 %fusion.1 = (f32[1,64,256]{2,1,0:T(8,128)}, f32[1,64,256]{2,1,0:T(8,128)}) fusion(f32[64,256]{1,0:T(8,128)S(1)} %get-tuple-element.7, f32[1,64,256]{2,1,0:T(8,128)S(1)} %copy-done.2, f32[1,64,256]{2,1,0:T(8,128)S(1)} %copy-done.1), kind=kLoop, calls=%fused_computation.2 | loop fusion | flops 114688 | bytes 327680 | tf_op jit(solution)/shard_map/broadcast_in_dim | solution.py:333
Async XLA Ops:
  0.6 56.6 %copy-start = (f32[64,256]{1,0:T(8,128)S(1)}, f32[64,256]{1,0:T(8,128)}, u32[]{:S(2)}) copy-start(f32[64,256]{1,0:T(8,128)} %anc.1) | copy-start | bytes 196612
  0.6 57.3 %copy-start.2 = (f32[1,64,256]{2,1,0:T(8,128)S(1)}, f32[1,64,256]{2,1,0:T(8,128)}, u32[]{:S(2)}) copy-start(f32[1,64,256]{2,1,0:T(8,128)} %sm.1) | copy-start | bytes 196612
  0.7 57.3 %copy-start.1 = (f32[1,64,256]{2,1,0:T(8,128)S(1)}, f32[1,64,256]{2,1,0:T(8,128)}, u32[]{:S(2)}) copy-start(f32[1,64,256]{2,1,0:T(8,128)} %fm.1) | copy-start | bytes 196612
  0.7 56.6 %copy-start.3 = (f32[64,256]{1,0:T(8,128)S(1)}, f32[64,256]{1,0:T(8,128)}, u32[]{:S(2)}) copy-start(f32[64,256]{1,0:T(8,128)} %param.13) | copy-start | bytes 196612
